TPU v7x, 32 devices: a whole 2x2x4 slice. The times are simulated.
32 devices in a mesh: grp: 2 (over x), tp: 4 (over y, core), dp: 4 (over z).
Axes of the slice: x: 2, y: 2, z: 4, core: 2. Of those that a mesh axis runs over, the one named last changes fastest.
Arguments:
- prompt: bfloat16 [8192, 8192], P(('grp', 'dp'), 'tp'), parts along dimension 0, may hold values from -6 to 6
- query_weight: bfloat16 [8192, 4096], P(None, 'tp'), may hold values from -0.0625 to 0.0625
- key_value_weight: bfloat16 [8192, 512], P(None, 'tp'), may hold values from -0.0625 to 0.0625
- adapter_down_weight: bfloat16 [8192, 64, 16], P('tp'), may hold values from -0.0625 to 0.0625
- query_up_weight: bfloat16 [64, 16, 4096], P(None, None, 'tp'), may hold values from -1.5 to 1.5
- adapter_up_weight: bfloat16 [64, 16, 512], P(None, None, 'tp'), may hold values from -1.5 to 1.5
- tenant: int32 [8192], P(('grp', 'dp')), parts along dimension 0, may hold values from 0 to 63
- page_destination_slot: int32 [512], P(('grp', 'dp')), parts along dimension 0, may hold values from 0 to 255, as said below
- key_value_cache: bfloat16 [8, 4, 256, 16, 256], P(('grp', 'dp'), 'tp'), parts along dimension 0, as said below
- queries: bfloat16 [8, 4, 16, 1024], P(('grp', 'dp'), 'tp'), parts along dimension 0, as said below
- request_page_table: int32 [256, 16], P(('grp', 'dp')), parts along dimension 0, may hold values from 0 to 287, as said below
- context_length: int32 [256], P(('grp', 'dp')), parts along dimension 0, may hold values from 33 to 256, as said below
Outputs:
- attention: bfloat16 [8, 4, 16, 1024], P(('grp', 'dp'), 'tp'), parts along dimension 0
- prompt_queries: bfloat16 [8192, 4096], P(('grp', 'dp'), 'tp'), parts along dimension 0
There are 2 independent parts, one for each index of `grp`. A program takes and returns all parts, laid end to end along the dimension named above; an argument that names none is the same for every part. Nothing has to cross between parts.
Inputs may be any that keep to these rules, and one draw needn't show every extreme that they name: `page_destination_slot`: A permutation. Entry p of replica i's 64 entries is o * 64 + s * 32 + q: page p of replica i goes to slot q of half s of replica o; every replica sends exactly 8 pages to each half of each replica. key_value_cache: entries of order one. queries: entries of order one for most requests; a few requests may hold much larger queries. `request_page_table`: entries below 256 are resident pages, 256 + q new slot q. A request using n pages has its last 2 used entries new, each new slot of a replica's half used by exactly one request; entries past the used pages are arbitrary pages. A request's pages in use are ceil(context_length / 16).
All inputs are finite; a program needn't handle non-finite values.
Results may differ from a plain program's by a relative error of at most 0.0062.
Values may be sent and summed in bfloat16 or wider, within the bound.
A program may use at most 128 MiB of HBM per device.

v0:
```python
import math

import jax
import jax.numpy as jnp
from jax import lax
from jax.sharding import PartitionSpec as P

PAGE = 16


def from_partner(value, axis, stride):
    mask = 2**stride
    pairs = [(source, source ^ mask) for source in range(lax.axis_size(axis))]
    return lax.ppermute(value, axis, pairs)


def choose_half(stacked, which_half):
    return lax.dynamic_index_in_dim(stacked, which_half, 1, keepdims=False)


def per_device(
    prompt,
    query_weight,
    key_value_weight,
    adapter_down_weight,
    query_up_weight,
    adapter_up_weight,
    tenant,
    page_destination_slot,
    key_value_cache,
    queries,
    request_page_table,
    context_length,
):
    token_count = prompt.shape[0]
    head_cols = key_value_weight.shape[1]
    query_cols = query_weight.shape[1]
    feature_part = lax.all_gather(prompt, "tp", axis=1, tiled=True)
    query_base = jnp.dot(feature_part, query_weight, preferred_element_type=jnp.float32)
    base_proj = jnp.dot(feature_part, key_value_weight, preferred_element_type=jnp.float32)
    tenant_total = adapter_down_weight.shape[1]
    adapter_rank_count = adapter_down_weight.shape[2]
    spread = jnp.dot(
        prompt,
        adapter_down_weight.reshape(
            adapter_down_weight.shape[0], tenant_total * adapter_rank_count
        ),
        preferred_element_type=jnp.float32,
    )
    onehot = (tenant[:, None] == jnp.arange(tenant_total)[None, :]).astype(jnp.float32)
    partial_value = jnp.sum(
        spread.reshape(token_count, tenant_total, adapter_rank_count) * onehot[:, :, None], axis=1
    )
    shrink = lax.psum(partial_value, "tp").astype(jnp.bfloat16)
    widened = (onehot.astype(jnp.bfloat16)[:, :, None] * shrink[:, None, :]).reshape(
        token_count, tenant_total * adapter_rank_count
    )
    joined_up_weight = jnp.concatenate([query_up_weight, adapter_up_weight], -1).reshape(
        tenant_total * adapter_rank_count, query_cols + head_cols
    )
    adapter_out = jnp.dot(widened, joined_up_weight, preferred_element_type=jnp.float32)
    prompt_queries = (query_base + 0.5 * adapter_out[:, :query_cols]).astype(jnp.bfloat16)
    own_pages = (
        (base_proj + 0.5 * adapter_out[:, query_cols:])
        .astype(jnp.bfloat16)
        .reshape(-1, PAGE, head_cols)
    )
    owners = lax.axis_size("dp")
    page_count = own_pages.shape[0]
    fresh_count = page_count // 2
    per_owner = page_count // (2 * owners)
    page_order = jnp.argsort(page_destination_slot)
    sorted_pages = own_pages[page_order].reshape(owners, 2, per_owner, PAGE, head_cols)
    slot_ids = (page_destination_slot[page_order] % fresh_count).reshape(owners, 2, per_owner)
    parity = lax.axis_index("tp") % 2
    arrived_both, slots_both = (
        lax.all_to_all(sorted_pages, "dp", split_axis=0, concat_axis=0, tiled=True),
        lax.all_to_all(slot_ids, "dp", split_axis=0, concat_axis=0, tiled=True),
    )
    partner = from_partner(choose_half(arrived_both, 1 - parity), "tp", 0)
    own_kind = choose_half(arrived_both, parity)
    arrived = jnp.where(
        parity == 0,
        jnp.concatenate([own_kind, partner], -1),
        jnp.concatenate([partner, own_kind], -1),
    )
    arrived_slots = choose_half(slots_both, parity)
    new_pages = jnp.zeros((fresh_count, PAGE, 2 * head_cols), jnp.bfloat16)
    new_pages = new_pages.at[arrived_slots.reshape(-1)].set(
        arrived.reshape(-1, PAGE, 2 * head_cols)
    )
    page_pool = jnp.concatenate([key_value_cache[0, 0], new_pages], 0)
    half_rows = queries.shape[2]
    row_table = lax.dynamic_slice_in_dim(request_page_table, parity * half_rows, half_rows, 0)
    lengths = lax.dynamic_slice_in_dim(context_length, parity * half_rows, half_rows, 0)
    gathered = page_pool[row_table].reshape(half_rows, -1, 2 * head_cols)
    key_part = gathered[..., :head_cols]
    value_part = gathered[..., head_cols:]
    query_part = queries[0, 0].reshape(half_rows, -1, head_cols)
    scores = jnp.einsum(
        "rgd,rcd->rgc", query_part, key_part, preferred_element_type=jnp.float32
    ) / math.sqrt(head_cols)
    position = jnp.arange(key_part.shape[1])
    scores = jnp.where(position[None, None, :] < lengths[:, None, None], scores, -jnp.inf)
    weights = jax.nn.softmax(scores, axis=-1).astype(jnp.bfloat16)
    attended = jnp.einsum("rgc,rcd->rgd", weights, value_part, preferred_element_type=jnp.float32)
    return (attended.reshape(1, 1, half_rows, -1).astype(jnp.bfloat16), prompt_queries)


def solution(mesh):
    in_specs = (
        P(("grp", "dp"), "tp"),
        P(None, "tp"),
        P(None, "tp"),
        P("tp", None, None),
        P(None, None, "tp"),
        P(None, None, "tp"),
        P(("grp", "dp")),
        P(("grp", "dp")),
        P(("grp", "dp"), "tp", None, None, None),
        P(("grp", "dp"), "tp", None, None),
        P(("grp", "dp"), None),
        P(("grp", "dp")),
    )
    out_specs = (P(("grp", "dp"), "tp", None, None), P(("grp", "dp"), "tp"))
    return jax.shard_map(
        per_device, mesh=mesh, in_specs=in_specs, out_specs=out_specs, check_vma=False
    )
```

profile of v0, /device:TPU:1, one launch (start us, length us, event | category | flops | bytes accessed | tf_op | source)
XLA Modules:
  0.0 188.7 jit_solution(12077812305142167403)
XLA Ops:
  7.3 0.7 all-gather.2.cloned.1.call-update
  8.0 2.0 %sort.17 = (s32[64]{0:T(128)}, s32[64]{0:T(128)S(1)}) sort(s32[64]{0:T(128)S(1)} %copy-done.1, s32[64]{0:T(128)S(1)} %iota.23), dimensions={0}, to_apply=%region_0.0 | sort | flops 384 | bytes 1024 | tf_op jit(solution)/shard_map/jit(argsort)/sort | solution.py:72
  10.0 0.8 gather_fusion
  10.9 0.6 and_select_fusion
  11.5 5.4 %all-to-all-start = ((s32[4,2,8]{2,1,0:T(2,128)}), s32[4,2,8]{2,1,0:T(2,128)S(1)}, u32[]{:S(2)}, u32[]{:S(2)}) async-start(s32[4,2,8]{2,1,0:T(2,128)} %and_select_fusion), calls=%async_computation | async-start | bytes 8192 | tf_op jit(solution)/shard_map/all_to_all | solution.py:78
  17.4 4.4 %copy.27 = bf16[64,16,1024]{2,0,1:T(8,128)(2,1)} copy(bf16[64,16,1024]{2,1,0:T(8,128)(2,1)} %param.16) | data formatting | bytes 4194304 | tf_op args[4]
  21.8 10.2 %multiply_reduce_fusion = f32[1024,16]{0,1:T(8,128)S(1)} fusion(bf16[64,16,2048]{2,1,0:T(8,128)(2,1)} %bitcast.44, bf16[1024,2048]{1,0:T(8,128)(2,1)} %param.12, f32[1024,64]{0,1:T(8,128)S(1)} %get-tuple-element.7), kind=kOutput, calls=%fused_computation.12 | convolution fusion | flops 4297048064 | bytes 8716288 | tf_op jit(solution)/shard_map/dot_general | solution.py:43
  32.0 12.8 %psum.7 = bf16[1024,16]{0,1:T(8,128)(2,1)S(1)} all-reduce(f32[1024,16]{0,1:T(8,128)S(1)} %multiply_reduce_fusion), channel_id=1, replica_groups=mesh['grp'=2,'tp'=4,'dp'=4] {'tp'}, use_global_device_ids=true, to_apply=%region_2.0 | all-reduce | flops 16384 | bytes 98304 | tf_op jit(solution)/shard_map/psum | solution.py:54
  44.8 6.2 %convolution_bitcast_fusion = f32[1024,1152]{1,0:T(8,128)} fusion(bf16[64,16,128]{2,0,1:T(8,128)(2,1)S(1)} %copy.28, bf16[64,16,1024]{2,0,1:T(8,128)(2,1)} %copy.27, bf16[1024,16]{0,1:T(8,128)(2,1)S(1)} %psum.7, bf16[1024,64]{0,1:T(8,128)(2,1)S(1)} %get-tuple-element.6), kind=kOutput, calls=%fused_computation.5 | convolution fusion | flops 2421686272 | bytes 7241728 | tf_op jit(solution)/shard_map/dot_general | solution.py:61
  51.0 68.1 %all-gather.2.cloned.1.call-done = bf16[1024,8192]{1,0:T(8,128)(2,1)} async-done(((bf16[1024,2048]{1,0:T(8,128)(2,1)}), bf16[1024,8192]{1,0:T(8,128)(2,1)}) %all-gather.2.cloned.1.call-update) | async-done | bytes 16777232 | tf_op jit(solution)/shard_map/all_gather | solution.py:38
  119.2 8.3 %fusion.14 = bf16[1024,128]{1,0:T(8,128)(2,1)S(1)} fusion(bf16[1024,8192]{1,0:T(8,128)(2,1)} %all-gather.2.cloned.1.call-done, bf16[8192,128]{1,0:T(8,128)(2,1)S(1)} %copy-done, f32[1024,1152]{1,0:T(8,128)} %convolution_bitcast_fusion), kind=kOutput, calls=%fused_computation.19 | convolution fusion | flops 2147876864 | bytes 19660800 | tf_op jit(solution)/shard_map/dot_general | solution.py:40
  127.5 1.3 gather_fusion.1
  128.8 4.3 %all-to-all-start.1 = ((bf16[4,2,8,16,128]{4,3,2,1,0:T(8,128)(2,1)}), bf16[4,2,8,16,128]{4,3,2,1,0:T(8,128)(2,1)S(1)}, u32[]{:S(2)}, u32[]{:S(2)}) async-start(bf16[4,2,8,16,128]{4,3,2,1,0:T(8,128)(2,1)} %bitcast.8), calls=%async_computation.1 | async-start | bytes 524288 | tf_op jit(solution)/shard_map/all_to_all | solution.py:77
  133.3 7.1 %all-to-all-done.1 = bf16[4,2,8,16,128]{4,3,2,1,0:T(8,128)(2,1)S(1)} async-done(((bf16[4,2,8,16,128]{4,3,2,1,0:T(8,128)(2,1)}), bf16[4,2,8,16,128]{4,3,2,1,0:T(8,128)(2,1)S(1)}, u32[]{:S(2)}, u32[]{:S(2)}) %all-to-all-start.1) | async-done | bytes 262176 | tf_op jit(solution)/shard_map/all_to_all | solution.py:77
  140.5 2.6 %collective-permute-start = (bf16[4,8,16,128]{3,2,1,0:T(8,128)(2,1)S(1)}, bf16[4,8,16,128]{3,2,1,0:T(8,128)(2,1)S(1)}, u32[]{:S(2)}, u32[]{:S(2)}) collective-permute-start(bf16[4,8,16,128]{3,2,1,0:T(8,128)(2,1)S(1)} %get-tuple-element.5), channel_id=1, source_target_pairs={{0,4},{4,0},{8,12},{12,8},{1,5},{5,1},{9,13},{13,9},{2,6},{6,2},{1... | collective-permute-start | bytes 393224 | tf_op jit(solution)/shard_map/ppermute | solution.py:14
  143.1 26.2 %fusion.2 = bf16[1024,1024]{1,0:T(8,128)(2,1)} fusion(f32[1024,1152]{1,0:T(8,128)} %convolution_bitcast_fusion, bf16[1024,8192]{1,0:T(8,128)(2,1)} %all-gather.2.cloned.1.call-done, bf16[8192,1024]{1,0:T(8,128)(2,1)} %param.13), kind=kOutput, calls=%fused_computation.8 | convolution fusion | flops 17183014912 | bytes 39845888 | tf_op jit(solution)/shard_map/dot_general | solution.py:39
  169.3 0.1 maximum_select_fusion
  169.4 1.5 scatter_fusion
  171.0 3.2 %pad_maximum_fusion = bf16[288,16,256]{2,1,0:T(8,128)(2,1)} fusion(bf16[32,16,256]{2,1,0:T(8,128)(2,1)S(1)} %scatter_fusion, bf16[256,16,256]{2,1,0:T(8,128)(2,1)} %bitcast.36), kind=kLoop, calls=%fused_computation.16 | loop fusion | flops 1179648 | bytes 4718592 | tf_op jit(solution)/shard_map/concatenate | solution.py:92
  174.2 3.7 %gather_fusion.2 = bf16[256,16,256]{2,1,0:T(8,128)(2,1)} fusion(bf16[288,16,256]{2,1,0:T(8,128)(2,1)} %pad_maximum_fusion, s32[1024]{0:T(1024)S(1)} %pad_clamp_fusion), kind=kCustom, calls=%fused_computation.2 | custom fusion | bytes 4195328 | tf_op jit(solution)/shard_map/gather | solution.py:96
  177.9 1.6 fusion.18
  179.5 0.2 fusion.29
  179.7 1.5 convolution_convert_fusion
  181.2 0.6 convert_element_type.49
  (35 shorter events, 0.8 us)
Async XLA Ops:
  7.2 112.0 %copy-start = (bf16[8192,128]{1,0:T(8,128)(2,1)S(1)}, bf16[8192,128]{1,0:T(8,128)(2,1)}, u32[]{:S(2)}) copy-start(bf16[8192,128]{1,0:T(8,128)(2,1)} %param.14) | copy-start | bytes 6291460
  7.2 0.8 copy-start.1
  7.2 9.8 %copy-start.6 = (s32[32]{0:T(128)S(1)}, s32[32]{0:T(128)}, u32[]{:S(2)}) copy-start(s32[32]{0:T(128)} %param.23) | copy-start | bytes 388
  7.2 9.8 %copy-start.4 = (s32[32,16]{0,1:T(8,128)S(1)}, s32[32,16]{0,1:T(8,128)}, u32[]{:S(2)}) copy-start(s32[32,16]{0,1:T(8,128)} %param.22) | copy-start | bytes 6148
  7.2 10.0 %copy-start.3 = (bf16[1,1,16,1024]{3,2,1,0:T(8,128)(2,1)S(1)}, bf16[1,1,16,1024]{3,2,1,0:T(8,128)(2,1)}, u32[]{:S(2)}) copy-start(bf16[1,1,16,1024]{3,2,1,0:T(8,128)(2,1)} %param.21) | copy-start | bytes 98308
  7.2 10.1 %copy-start.2 = (bf16[64,16,128]{2,1,0:T(8,128)(2,1)S(1)}, bf16[64,16,128]{2,1,0:T(8,128)(2,1)}, u32[]{:S(2)}) copy-start(bf16[64,16,128]{2,1,0:T(8,128)(2,1)} %param.17) | copy-start | bytes 786436
  7.2 14.5 %copy-start.5 = (s32[1024]{0:T(1024)S(1)}, s32[1024]{0:T(1024)}, u32[]{:S(2)}) copy-start(s32[1024]{0:T(1024)} %param.18) | copy-start | bytes 12292
  7.2 111.9 %all-gather.2.cloned.1.call-start = ((), (), s32[]{:S(2)}) async-start(), calls=%async_computation.2 | async-start | bytes 20971520 | tf_op jit(solution)/shard_map/all_gather | solution.py:38
  11.5 117.3 %all-to-all-start = ((s32[4,2,8]{2,1,0:T(2,128)}), s32[4,2,8]{2,1,0:T(2,128)S(1)}, u32[]{:S(2)}, u32[]{:S(2)}) async-start(s32[4,2,8]{2,1,0:T(2,128)} %and_select_fusion), calls=%async_computation | async-start | bytes 8192 | tf_op jit(solution)/shard_map/all_to_all | solution.py:78
  128.8 11.6 %all-to-all-start.1 = ((bf16[4,2,8,16,128]{4,3,2,1,0:T(8,128)(2,1)}), bf16[4,2,8,16,128]{4,3,2,1,0:T(8,128)(2,1)S(1)}, u32[]{:S(2)}, u32[]{:S(2)}) async-start(bf16[4,2,8,16,128]{4,3,2,1,0:T(8,128)(2,1)} %bitcast.8), calls=%async_computation.1 | async-start | bytes 524288 | tf_op jit(solution)/shard_map/all_to_all | solution.py:77
  140.5 28.8 %collective-permute-start = (bf16[4,8,16,128]{3,2,1,0:T(8,128)(2,1)S(1)}, bf16[4,8,16,128]{3,2,1,0:T(8,128)(2,1)S(1)}, u32[]{:S(2)}, u32[]{:S(2)}) collective-permute-start(bf16[4,8,16,128]{3,2,1,0:T(8,128)(2,1)S(1)} %get-tuple-element.5), channel_id=1, source_target_pairs={{0,4},{4,0},{8,12},{12,8},{1,5},{5,1},{9,13},{13,9},{2,6},{6,2},{1... | collective-permute-start | bytes 393224 | tf_op jit(solution)/shard_map/ppermute | solution.py:14
Sparse Core Ops, SparseCore 0:
  9.6 109.4 all-gather.1
where the time goes:
time: 189 us
  waiting for transfers between devices  75.9 us (40%)
  matrix products  54 us (29%)
  between operations  14.2 us (8%)
  local copies, waits for them, and re-layouts  13 us (7%)
  blocking collectives  12.8 us (7%)
  starting transfers between devices  12.4 us (7%)
  other arithmetic  6.38 us (3%)
    all_gather x1, waiting for transfers between devices, per_device(): feature_part = lax.all_gather(prompt, 'tp', axis=1, tiled=True)  68.1 us
    dot_general x1, matrix products, per_device(): jnp.dot(feature_part, query_weight, preferred_element_type=jnp.float32)  26.2 us
    psum x1, blocking collectives, per_device(): shrink = lax.psum(partial_value, 'tp').astype(jnp.bfloat16)  12.8 us
    dot_general x1, matrix products, per_device(): jnp.dot(prompt, adapter_down_weight.reshape(adapter_down_weight.shape[0],...  10.2 us
    dot_general x1, matrix products, per_device(): jnp.dot(feature_part, key_value_weight, preferred_element_type=jnp.float32)  8.33 us
    all_to_all x1, waiting for transfers between devices, per_device(): lax.all_to_all(sorted_pages, 'dp', split_axis=0, concat_axis=0, tiled=True)  7.11 us
    dot_general x1, matrix products, per_device(): jnp.dot(widened, joined_up_weight, preferred_element_type=jnp.float32)  6.17 us
    all_to_all x1, starting transfers between devices, per_device(): lax.all_to_all(slot_ids, 'dp', split_axis=0, concat_axis=0, tiled=True)  5.42 us
  transfers between devices with their start and end apart: 4, of which 2 were waited for; matrix products, arithmetic and copies ran while one was open for 32% of the time, Pallas kernels for 0%

commit v1 on v0

v1 whole, which is shorter than its diff:
```python
import functools
import math

import jax
import jax.numpy as jnp
from jax import lax
from jax.experimental import pallas as pl
from jax.experimental.pallas import tpu as pltpu
from jax.sharding import PartitionSpec as P

PAGE = 16
CHUNK = 128
BLOCK = 1024
NEG = -1e30
F32 = jnp.float32
BF16 = jnp.bfloat16


def nt_dot(a, b):
    return lax.dot_general(a, b, (((1,), (1,)), ((), ())), preferred_element_type=F32)


def dot(a, b):
    return jnp.dot(a, b, preferred_element_type=F32)


def kernel(
    n_tp,
    n_dp,
    pool,
    x_hbm,
    wq_hbm,
    wkv_hbm,
    wd_hbm,
    wup_hbm,
    wkup_hbm,
    tenant,
    slots,
    meta,
    cache_hbm,
    queries,
    out_a,
    out_q,
    xg,
    wq,
    wkv,
    wd,
    wup,
    wkup,
    cache,
    oq,
    kv,
    shp,
    shrink,
    slots_all,
    counts,
    qs,
    o_acc,
    m_acc,
    l_acc,
    acc_q,
    load_sem,
    xload_sem,
    sib_send,
    sib_recv,
    far_send,
    far_recv,
    fwd_send,
    fwd_recv,
    shr_send,
    shr_recv,
    slot_send,
    slot_recv,
    page_send,
    page_recv,
    out_sem,
):
    me = lax.axis_index("tp")
    dp = lax.axis_index("dp")
    kind = lax.rem(me, 2)
    sib = me + 1 - 2 * kind
    tok = x_hbm.shape[0]
    n_chunk = tok // CHUNK
    n_y = n_tp // 2
    tenants = wd.shape[0] // 16

    def rows(k):
        return pl.ds(pl.multiple_of(k * CHUNK, CHUNK), CHUNK)

    def remote(src, dst, ss, rs, tp_id, dp_id):
        return pltpu.make_async_remote_copy(
            src_ref=src,
            dst_ref=dst,
            send_sem=ss,
            recv_sem=rs,
            device_id={"tp": tp_id, "dp": dp_id},
            device_id_type=pl.DeviceIdType.MESH,
        )

    barrier = pltpu.get_barrier_semaphore()
    n_peers = n_tp - 1 + 2 * (n_dp - 1)
    for d in range(1, n_tp):
        pl.semaphore_signal(
            barrier,
            inc=1,
            device_id={"tp": lax.rem(me + d, n_tp), "dp": dp},
            device_id_type=pl.DeviceIdType.MESH,
        )
    for d in range(1, n_dp):
        for t in (me, sib):
            pl.semaphore_signal(
                barrier,
                inc=1,
                device_id={"tp": t, "dp": lax.rem(dp + d, n_dp)},
                device_id_type=pl.DeviceIdType.MESH,
            )

    own_load = pltpu.make_async_copy(x_hbm, xg.at[me], xload_sem)
    own_load.start()
    loads = [
        pltpu.make_async_copy(src, dst, load_sem.at[i])
        for i, (src, dst) in enumerate(
            (
                (wd_hbm, wd),
                (cache_hbm, cache),
                (wkv_hbm, wkv),
                (wup_hbm, wup),
                (wkup_hbm, wkup),
                (wq_hbm, wq),
            )
        )
    ]
    for load in loads:
        load.start()

    pl.semaphore_wait(barrier, n_peers)

    def to_sibling(k):
        return remote(
            x_hbm.at[rows(k)], xg.at[me, rows(k)], sib_send.at[k], sib_recv.at[k], sib, dp
        )

    def from_sibling(k):
        return remote(
            x_hbm.at[rows(k)], xg.at[sib, rows(k)], sib_send.at[k], sib_recv.at[k], sib, dp
        )

    def far_to(y):
        return lax.rem(me + 2 * y, n_tp)

    def far_from(y):
        return lax.rem(me + n_tp - 2 * y, n_tp)

    def to_far(k, y):
        return remote(
            x_hbm.at[rows(k)],
            xg.at[me, rows(k)],
            far_send.at[k, y - 1],
            far_recv.at[k, y - 1],
            far_to(y),
            dp,
        )

    def from_far(k, y):
        return remote(
            x_hbm.at[rows(k)],
            xg.at[far_from(y), rows(k)],
            far_send.at[k, y - 1],
            far_recv.at[k, y - 1],
            far_to(y),
            dp,
        )

    def pass_on(k, y):
        block = xg.at[far_from(y), rows(k)]
        return remote(block, block, fwd_send.at[k, y - 1], fwd_recv.at[k, y - 1], sib, dp)

    def passed(k, y):
        src = lax.rem(sib + n_tp - 2 * y, n_tp)
        block = xg.at[src, rows(k)]
        return remote(block, block, fwd_send.at[k, y - 1], fwd_recv.at[k, y - 1], sib, dp)

    def to_shrink(d):
        return remote(
            shp.at[me],
            shp.at[me],
            shr_send.at[d - 1],
            shr_recv.at[d - 1],
            lax.rem(me + d, n_tp),
            dp,
        )

    def from_shrink(d):
        src = lax.rem(me + n_tp - d, n_tp)
        return remote(shp.at[src], shp.at[src], shr_send.at[d - 1], shr_recv.at[d - 1], src, dp)

    def to_slots(d):
        return remote(
            slots,
            slots_all.at[dp],
            slot_send.at[d - 1],
            slot_recv.at[d - 1],
            me,
            lax.rem(dp + d, n_dp),
        )

    def from_slots(d):
        src = lax.rem(dp + n_dp - d, n_dp)
        return remote(
            slots, slots_all.at[src], slot_send.at[d - 1], slot_recv.at[d - 1], me, src
        )

    def page_copy(k, which, other, d, replica, target_tp, target_dp):
        block = kv.at[which, replica, rows(k)]
        index = other * n_dp + d
        return remote(
            block, block, page_send.at[k, index], page_recv.at[k, index], target_tp, target_dp
        )

    def page_pairs():
        return [(other, d) for other in (0, 1) for d in range(n_dp) if other or d]

    def to_pages(k, other, d):
        target = sib if other else me
        return page_copy(k, kind, other, d, dp, target, lax.rem(dp + d, n_dp))

    def from_pages(k, other, d):
        which = 1 - kind if other else kind
        src = lax.rem(dp + n_dp - d, n_dp)
        return page_copy(k, which, other, d, src, sib, src)

    for k in range(2):
        for y in range(1, n_y):
            to_far(k, y).start()

    @pl.loop(0, n_chunk)
    def _(k):
        to_sibling(k).start()

    for d in range(1, n_dp):
        to_slots(d).start()
    slots_all[dp] = slots[...]

    own_load.wait()
    loads[0].wait()
    wide = 2 * CHUNK

    @pl.loop(0, tok // wide)
    def _(b):
        cols = pl.ds(pl.multiple_of(b * wide, wide), wide)
        spread = nt_dot(wd[...], xg[me, cols, :])
        group = lax.broadcasted_iota(jnp.int32, spread.shape, 0) // 16
        kept = jnp.where(group == tenant[:, cols], spread, 0.0)
        shp[me, :, cols] = jnp.sum(kept.reshape(tenants, 16, wide), axis=0)

    for d in range(1, n_tp):
        to_shrink(d).start()

    lengths = meta[pl.ds(pl.multiple_of(kind * 16, 16), 16), 16:17]
    table = meta[pl.ds(pl.multiple_of(kind * 16, 16), 16), 0:16]
    inv_scale = 1.0 / math.sqrt(128)

    def count_of(page_ids):
        lane = lax.broadcasted_iota(jnp.int32, (16, BLOCK), 1)
        offset = lane % PAGE
        total = jnp.zeros((16, BLOCK), F32)
        for p in range(16):
            hit = (table[:, p : p + 1] == page_ids) & (offset + p * PAGE < lengths)
            total += jnp.where(hit, 1.0, 0.0)
        return total

    def scores_of(keys, count):
        s = nt_dot(qs[...], keys).reshape(8, 16, BLOCK) * inv_scale
        return jnp.where(count[None] > 0, s, NEG)

    def weigh(s, count, m, values):
        p = count[None] * jnp.exp(s - m)
        l = jnp.sum(p, axis=2, keepdims=True)
        o = dot(p.reshape(128, BLOCK).astype(BF16), values)
        return l, o.reshape(8, 16, 128)

    for g in range(8):
        qs[g * 16 : (g + 1) * 16, :] = queries[:, g * 128 : (g + 1) * 128]
    m_acc[...] = jnp.full(m_acc.shape, NEG, F32)
    l_acc[...] = jnp.zeros(l_acc.shape, F32)
    o_acc[...] = jnp.zeros(o_acc.shape, F32)
    loads[1].wait()

    @pl.loop(0, pool * PAGE // BLOCK)
    def _(b):
        cols = pl.ds(pl.multiple_of(b * BLOCK, BLOCK), BLOCK)
        lane = lax.broadcasted_iota(jnp.int32, (16, BLOCK), 1)
        count = count_of((lane + b * BLOCK) // PAGE)
        s = scores_of(cache[cols, :128], count)
        m_old = m_acc[...]
        m = jnp.maximum(m_old, jnp.max(s, axis=2, keepdims=True))
        l, o = weigh(s, count, m, cache[cols, 128:])
        alpha = jnp.exp(m_old - m)
        m_acc[...] = m
        l_acc[...] = l_acc[...] * alpha + l
        o_acc[...] = o_acc[...] * alpha + o

    for d in range(1, n_dp):
        from_slots(d).wait_recv()
    new_pages = tok // PAGE // 2

    @pl.loop(0, n_dp)
    def _(i):
        dest = slots_all[i, 0:1, :]
        mine = dest // new_pages == dp * 2 + kind
        page_ids = jnp.where(mine, dest % new_pages + pool, -1)
        counts[i] = count_of(page_ids)

    for d in range(1, n_tp):
        from_shrink(d).wait_recv()
    total = shp[0]
    for t in range(1, n_tp):
        total = total + shp[t]
    shrink[...] = total.astype(BF16).astype(F32)
    for load in loads[2:]:
        load.wait()

    @pl.loop(0, n_chunk)
    def _(k):
        cols = rows(k)
        from_sibling(k).wait_recv()
        low = jnp.broadcast_to(shrink[:, cols][None], (tenants, 16, CHUNK))
        low = low.reshape(tenants * 16, CHUNK)
        group = lax.broadcasted_iota(jnp.int32, low.shape, 0) // 16
        widened = jnp.where(group == tenant[:, cols], low, 0.0).T.astype(BF16)
        acc_kv = 0.5 * dot(widened, wkup[...])
        acc_q[...] = 0.5 * dot(widened, wup[...])
        for src in (me, sib):
            acc_kv += dot(xg[src, cols, :], wkv[src])
            acc_q[...] += dot(xg[src, cols, :], wq[src])
        for y in range(1, n_y):
            from_far(k, y).wait_recv()
            pass_on(k, y).start()

        @pl.when(k + 2 < n_chunk)
        def _():
            for y in range(1, n_y):
                to_far(k + 2, y).start()

        for y in range(1, n_y):
            src = far_from(y)
            acc_kv += dot(xg[src, cols, :], wkv[src])
        for y in range(1, n_y):
            passed(k, y).wait_recv()
            src = lax.rem(sib + n_tp - 2 * y, n_tp)
            acc_kv += dot(xg[src, cols, :], wkv[src])
        kv[kind, dp, cols, :] = acc_kv.astype(BF16)
        for other, d in page_pairs():
            to_pages(k, other, d).start()
        for y in range(1, n_y):
            for base in (me, sib):
                src = lax.rem(base + n_tp - 2 * y, n_tp)
                acc_q[...] += dot(xg[src, cols, :], wq[src])
        oq[cols, :] = acc_q[...].astype(BF16)
        pltpu.make_async_copy(oq.at[cols], out_q.at[cols], out_sem.at[k]).start()

    @pl.loop(0, n_chunk)
    def _(k):
        for other, d in page_pairs():
            from_pages(k, other, d).wait_recv()

    parts = [scores_of(kv[0, i], counts[i]) for i in range(n_dp)]
    m_old = m_acc[...]
    m = m_old
    for s in parts:
        m = jnp.maximum(m, jnp.max(s, axis=2, keepdims=True))
    alpha = jnp.exp(m_old - m)
    l_sum = l_acc[...] * alpha
    o_sum = o_acc[...] * alpha
    for i, s in enumerate(parts):
        l, o = weigh(s, counts[i], m, kv[1, i])
        l_sum += l
        o_sum += o
    result = (o_sum / l_sum).astype(BF16)
    for g in range(8):
        out_a[:, g * 128 : (g + 1) * 128] = result[g]

    for d in range(1, n_dp):
        to_slots(d).wait_send()
    for d in range(1, n_tp):
        to_shrink(d).wait_send()

    @pl.loop(0, n_chunk)
    def _(k):
        to_sibling(k).wait_send()
        for y in range(1, n_y):
            to_far(k, y).wait_send()
            pass_on(k, y).wait_send()
        for other, d in page_pairs():
            to_pages(k, other, d).wait_send()
        pltpu.make_async_copy(oq.at[rows(k)], out_q.at[rows(k)], out_sem.at[k]).wait()


def per_device(
    n_tp,
    n_dp,
    prompt,
    query_weight,
    key_value_weight,
    adapter_down_weight,
    query_up_weight,
    adapter_up_weight,
    tenant,
    page_destination_slot,
    key_value_cache,
    queries,
    request_page_table,
    context_length,
):
    tok, feat = prompt.shape
    head = key_value_weight.shape[1]
    qcols = query_weight.shape[1]
    tenants, rank = adapter_down_weight.shape[1:]
    ranks = tenants * rank
    pool = key_value_cache.shape[2]
    half = queries.shape[2]
    n_chunk = tok // CHUNK
    down = adapter_down_weight.transpose(1, 2, 0).reshape(ranks, feat)
    slots = jnp.broadcast_to(jnp.repeat(page_destination_slot, PAGE)[None, :], (8, tok))
    meta = jnp.concatenate([request_page_table, context_length[:, None]], axis=1)
    hbm = pl.BlockSpec(memory_space=pl.ANY)
    vmem = pl.BlockSpec(memory_space=pltpu.VMEM)
    dma = pltpu.SemaphoreType.DMA
    n_far = n_tp // 2 - 1
    out_a, out_q = pl.pallas_call(
        functools.partial(kernel, n_tp, n_dp, pool),
        out_shape=(
            jax.ShapeDtypeStruct((half, queries.shape[3]), BF16),
            jax.ShapeDtypeStruct((tok, qcols), BF16),
        ),
        in_specs=[hbm] * 6 + [vmem] * 3 + [hbm, vmem],
        out_specs=(vmem, hbm),
        scratch_shapes=[
            pltpu.VMEM((n_tp, tok, feat), BF16),
            pltpu.VMEM((n_tp, feat, qcols), BF16),
            pltpu.VMEM((n_tp, feat, head), BF16),
            pltpu.VMEM((ranks, feat), BF16),
            pltpu.VMEM((ranks, qcols), BF16),
            pltpu.VMEM((ranks, head), BF16),
            pltpu.VMEM((pool * PAGE, 2 * head), BF16),
            pltpu.VMEM((tok, qcols), BF16),
            pltpu.VMEM((2, n_dp, tok, head), BF16),
            pltpu.VMEM((n_tp, rank, tok), F32),
            pltpu.VMEM((rank, tok), F32),
            pltpu.VMEM((n_dp, 8, tok), jnp.int32),
            pltpu.VMEM((n_dp, half, tok), F32),
            pltpu.VMEM((8 * half, head), BF16),
            pltpu.VMEM((8, half, head), F32),
            pltpu.VMEM((8, half, 1), F32),
            pltpu.VMEM((8, half, 1), F32),
            pltpu.VMEM((CHUNK, qcols), F32),
            dma((6,)),
            dma,
            dma((n_chunk,)),
            dma((n_chunk,)),
            dma((n_chunk, n_far)),
            dma((n_chunk, n_far)),
            dma((n_chunk, n_far)),
            dma((n_chunk, n_far)),
            dma((n_tp - 1,)),
            dma((n_tp - 1,)),
            dma((n_dp - 1,)),
            dma((n_dp - 1,)),
            dma((n_chunk, 2 * n_dp)),
            dma((n_chunk, 2 * n_dp)),
            dma((n_chunk,)),
        ],
        compiler_params=pltpu.CompilerParams(
            collective_id=0, has_side_effects=True, vmem_limit_bytes=63 * 2**20
        ),
        name="serve_layer",
    )(
        prompt,
        query_weight.reshape(n_tp, feat, qcols),
        key_value_weight.reshape(n_tp, feat, head),
        down,
        query_up_weight.reshape(ranks, qcols),
        adapter_up_weight.reshape(ranks, head),
        tenant[None, :],
        slots,
        meta,
        key_value_cache.reshape(pool * PAGE, 2 * head),
        queries.reshape(half, -1),
    )
    return out_a.reshape(1, 1, half, -1), out_q


def solution(mesh):
    in_specs = (
        P(("grp", "dp"), "tp"),
        P(None, "tp"),
        P(None, "tp"),
        P("tp", None, None),
        P(None, None, "tp"),
        P(None, None, "tp"),
        P(("grp", "dp")),
        P(("grp", "dp")),
        P(("grp", "dp"), "tp", None, None, None),
        P(("grp", "dp"), "tp", None, None),
        P(("grp", "dp"), None),
        P(("grp", "dp")),
    )
    out_specs = (P(("grp", "dp"), "tp", None, None), P(("grp", "dp"), "tp"))
    return jax.shard_map(
        functools.partial(per_device, mesh.shape["tp"], mesh.shape["dp"]),
        mesh=mesh,
        in_specs=in_specs,
        out_specs=out_specs,
        check_vma=False,
    )
```

time: 189 us -> 125 us (0.66)
  Pallas kernels: 0 us -> 116 us
  waiting for transfers between devices: 75.9 us -> 0 us
  matrix products: 54 us -> 0 us
  between operations: 14.2 us -> 0.64 us
  blocking collectives: 12.8 us -> 0 us
  starting transfers between devices: 12.4 us -> 0 us
  other arithmetic: 6.38 us -> 0.68 us
  local copies, waits for them, and re-layouts: 13 us -> 7.39 us
    pallas_call x0 -> x1, Pallas kernels: none -> 116 us  [per_device(): pl.pallas_call(functools.partial(kernel, n_tp, n_dp, pool), out_shape=(ja...]
    all_gather x1 -> x0, waiting for transfers between devices: 68.1 us -> none  [per_device(): feature_part = lax.all_gather(prompt, 'tp', axis=1, tiled=True)]
    dot_general x6 -> x0, matrix products: 54 us -> none  [the longest x1 26.2 us: per_device(): jnp.dot(feature_part, query_weight, preferred_element_type=jnp.float32)]
    psum x1 -> x0, blocking collectives: 12.8 us -> none  [per_device(): shrink = lax.psum(partial_value, 'tp').astype(jnp.bfloat16)]
    all_to_all x2 -> x0, starting transfers between devices: 9.74 us -> none  [the longest x1 5.42 us: per_device(): lax.all_to_all(slot_ids, 'dp', split_axis=0, concat_axis=0, tiled=True)]
    all_to_all x2 -> x0, waiting for transfers between devices: 7.11 us -> none  [the longest x1 7.11 us: per_device(): lax.all_to_all(sorted_pages, 'dp', split_axis=0, concat_axis=0, tiled=True)]
    gather x4 -> x0, local copies, waits for them, and re-layouts: 5.92 us -> none  [the longest x1 3.73 us: per_device(): gathered = page_pool[row_table].reshape(half_rows, -1, 2 * head_cols)]
    ppermute x1 -> x0, starting transfers between devices: 2.61 us -> none  [from_partner(): return lax.ppermute(value, axis, pairs)]
  transfers between devices with their start and end apart: 4 -> 0, of which waited for: 2 -> 0; matrix products, arithmetic and copies ran while one was open for 32% -> 0% of each run, Pallas kernels for 0% -> 0%
where the time goes in v1:
time: 125 us
  Pallas kernels  116 us (93%)
  local copies, waits for them, and re-layouts  7.39 us (6%)
    pallas_call x1, Pallas kernels, per_device(): pl.pallas_call(functools.partial(kernel, n_tp, n_dp, pool), out_shape=(ja...  116 us
    unnamed x3, local copies, waits for them, and re-layouts  5.23 us

profile of v1, /device:TPU:1, one launch (start us, length us, event | category | flops | bytes accessed | tf_op | source)
XLA Modules:
  0.0 125.1 jit_solution(7455567505161914897)
XLA Ops:
  0.6 0.8 copy.16
  1.4 0.7 copy.17
  2.1 0.7 pad_add_fusion.meta
  2.8 0.7 broadcast_in_dim.17
  3.5 0.1 broadcast_in_dim.18
  3.6 0.6 broadcast_in_dim.19.slots
  4.3 116.4 %serve_layer.1 = (bf16[16,1024]{1,0:T(8,128)(2,1)}, bf16[1024,1024]{1,0:T(8,128)(2,1)}) custom-call(bf16[1024,2048]{1,0:T(8,128)(2,1)} %x_hbm.1, bf16[4,2048,1024]{2,1,0:T(8,128)(2,1)} %bitcast.12, bf16[4,2048,128]{2,1,0:T(8,128)(2,1)} %bitcast.14, bf16[1024,2048]{1,0:T(8,128)(2,1)} %bitcast.13, bf16[1024,1024]{1,0:T(8,128)(2,1)} %bitcast.15, ...), custom_call_target="tpu_custom_call" | custom-call | tf_op jit(solution)/shard_map/serve_layer/pallas_call | solution.py:430
  120.7 1.4 %copy.20 = bf16[1,1,16,1024]{3,2,1,0:T(8,128)(2,1)} copy(bf16[1,1,16,1024]{3,2,1,0:T(8,128)(2,1)} %bitcast.18) | data formatting | bytes 65536
  122.0 3.1 %copy.21 = bf16[1024,1024]{1,0:T(8,128)(2,1)} copy(bf16[1024,1024]{1,0:T(8,128)(2,1)} %get-tuple-element.9) | data formatting | bytes 4194304

commit v2 on v1

--- a/solution.py
+++ b/solution.py
@@ -10,6 +10,8 @@
 
 PAGE = 16
 CHUNK = 128
+SUB = 32
+AHEAD = 3
 BLOCK = 1024
 NEG = -1e30
 F32 = jnp.float32
@@ -18,6 +20,16 @@
 
 def nt_dot(a, b):
     return lax.dot_general(a, b, (((1,), (1,)), ((), ())), preferred_element_type=F32)
+
+
+def exact_nt(a, b):
+    return lax.dot_general(
+        a,
+        b,
+        (((1,), (1,)), ((), ())),
+        preferred_element_type=F32,
+        precision=lax.Precision.HIGHEST,
+    )
 
 
 def dot(a, b):
@@ -36,7 +48,8 @@
     wkup_hbm,
     tenant,
     slots,
-    meta,
+    table_t,
+    context,
     cache_hbm,
     queries,
     out_a,
@@ -50,9 +63,11 @@
     cache,
     oq,
     kv,
+    pair,
     shp,
     shrink,
     slots_all,
+    slots_own,
     counts,
     qs,
     o_acc,
@@ -67,6 +82,8 @@
     far_recv,
     fwd_send,
     fwd_recv,
+    pair_send,
+    pair_recv,
     shr_send,
     shr_recv,
     slot_send,
@@ -84,8 +101,16 @@
     n_y = n_tp // 2
     tenants = wd.shape[0] // 16
 
+    n_sub = CHUNK // SUB
+    last = n_chunk - 1
+
     def rows(k):
         return pl.ds(pl.multiple_of(k * CHUNK, CHUNK), CHUNK)
+
+    def unit_rows(k):
+        if isinstance(k, int) and k >= last:
+            return pl.ds(last * CHUNK + (k - last) * SUB, SUB)
+        return rows(k)
 
     def remote(src, dst, ss, rs, tp_id, dp_id):
         return pltpu.make_async_remote_copy(
@@ -153,8 +178,8 @@
 
     def to_far(k, y):
         return remote(
-            x_hbm.at[rows(k)],
-            xg.at[me, rows(k)],
+            x_hbm.at[unit_rows(k)],
+            xg.at[me, unit_rows(k)],
             far_send.at[k, y - 1],
             far_recv.at[k, y - 1],
             far_to(y),
@@ -163,8 +188,8 @@
 
     def from_far(k, y):
         return remote(
-            x_hbm.at[rows(k)],
-            xg.at[far_from(y), rows(k)],
+            x_hbm.at[unit_rows(k)],
+            xg.at[far_from(y), unit_rows(k)],
             far_send.at[k, y - 1],
             far_recv.at[k, y - 1],
             far_to(y),
@@ -172,31 +197,40 @@
         )
 
     def pass_on(k, y):
-        block = xg.at[far_from(y), rows(k)]
+        block = xg.at[far_from(y), unit_rows(k)]
         return remote(block, block, fwd_send.at[k, y - 1], fwd_recv.at[k, y - 1], sib, dp)
 
     def passed(k, y):
         src = lax.rem(sib + n_tp - 2 * y, n_tp)
-        block = xg.at[src, rows(k)]
+        block = xg.at[src, unit_rows(k)]
         return remote(block, block, fwd_send.at[k, y - 1], fwd_recv.at[k, y - 1], sib, dp)
 
-    def to_shrink(d):
-        return remote(
-            shp.at[me],
-            shp.at[me],
-            shr_send.at[d - 1],
-            shr_recv.at[d - 1],
-            lax.rem(me + d, n_tp),
-            dp,
-        )
-
-    def from_shrink(d):
-        src = lax.rem(me + n_tp - d, n_tp)
-        return remote(shp.at[src], shp.at[src], shr_send.at[d - 1], shr_recv.at[d - 1], src, dp)
+    my_y = me // 2
+    span = tok // 2
+
+    def part(c):
+        return pl.ds(pl.multiple_of(c * span, span), span)
+
+    def swap_shrink(c):
+        block = pair.at[c]
+        return remote(block, block, pair_send, pair_recv, sib, dp)
+
+    def to_shrink(y, other):
+        block = shp.at[my_y, :, part(kind)]
+        target = lax.rem((sib if other else me) + 2 * y, n_tp)
+        index = 2 * (y - 1) + other
+        return remote(block, block, shr_send.at[index], shr_recv.at[index], target, dp)
+
+    def from_shrink(y, other):
+        source = lax.rem((sib if other else me) + n_tp - 2 * y, n_tp)
+        half = 1 - kind if other else kind
+        block = shp.at[lax.rem(my_y + n_y - y, n_y), :, part(half)]
+        index = 2 * (y - 1) + other
+        return remote(block, block, shr_send.at[index], shr_recv.at[index], source, dp)
 
     def to_slots(d):
         return remote(
-            slots,
+            slots_own,
             slots_all.at[dp],
             slot_send.at[d - 1],
             slot_recv.at[d - 1],
@@ -207,11 +241,11 @@
     def from_slots(d):
         src = lax.rem(dp + n_dp - d, n_dp)
         return remote(
-            slots, slots_all.at[src], slot_send.at[d - 1], slot_recv.at[d - 1], me, src
+            slots_own, slots_all.at[src], slot_send.at[d - 1], slot_recv.at[d - 1], me, src
         )
 
     def page_copy(k, which, other, d, replica, target_tp, target_dp):
-        block = kv.at[which, replica, rows(k)]
+        block = kv.at[which, replica, unit_rows(k)]
         index = other * n_dp + d
         return remote(
             block, block, page_send.at[k, index], page_recv.at[k, index], target_tp, target_dp
@@ -229,7 +263,7 @@
         src = lax.rem(dp + n_dp - d, n_dp)
         return page_copy(k, which, other, d, src, sib, src)
 
-    for k in range(2):
+    for k in range(AHEAD):
         for y in range(1, n_y):
             to_far(k, y).start()
 
@@ -237,9 +271,12 @@
     def _(k):
         to_sibling(k).start()
 
+    n_pages = slots.shape[1]
+    slots_own[...] = jnp.zeros(slots_own.shape, jnp.int32)
+    slots_own[0:1, 0:n_pages] = slots[...]
     for d in range(1, n_dp):
         to_slots(d).start()
-    slots_all[dp] = slots[...]
+    slots_all[dp] = slots_own[...]
 
     own_load.wait()
     loads[0].wait()
@@ -251,13 +288,15 @@
         spread = nt_dot(wd[...], xg[me, cols, :])
         group = lax.broadcasted_iota(jnp.int32, spread.shape, 0) // 16
         kept = jnp.where(group == tenant[:, cols], spread, 0.0)
-        shp[me, :, cols] = jnp.sum(kept.reshape(tenants, 16, wide), axis=0)
-
-    for d in range(1, n_tp):
-        to_shrink(d).start()
-
-    lengths = meta[pl.ds(pl.multiple_of(kind * 16, 16), 16), 16:17]
-    table = meta[pl.ds(pl.multiple_of(kind * 16, 16), 16), 0:16]
+        pair[kind, :, cols] = jnp.sum(kept.reshape(tenants, 16, wide), axis=0)
+
+    swap_shrink(kind).start()
+
+    pick = lax.broadcasted_iota(jnp.int32, (16, table_t.shape[1]), 1)
+    pick = jnp.where(pick == lax.broadcasted_iota(jnp.int32, pick.shape, 0) + kind * 16, 1.0, 0.0)
+    table = exact_nt(pick, table_t[...].astype(F32)).astype(jnp.int32)
+    length_rows = jnp.broadcast_to(context[...].astype(F32), pick.shape)
+    lengths = exact_nt(pick, length_rows)[:, 0:1].astype(jnp.int32)
     inv_scale = 1.0 / math.sqrt(128)
 
     def count_of(page_ids):
@@ -270,14 +309,36 @@
         return total
 
     def scores_of(keys, count):
-        s = nt_dot(qs[...], keys).reshape(8, 16, BLOCK) * inv_scale
+        s = nt_dot(qs[...], keys).reshape(8, 16, count.shape[1]) * inv_scale
         return jnp.where(count[None] > 0, s, NEG)
 
     def weigh(s, count, m, values):
         p = count[None] * jnp.exp(s - m)
         l = jnp.sum(p, axis=2, keepdims=True)
-        o = dot(p.reshape(128, BLOCK).astype(BF16), values)
+        o = dot(p.reshape(128, count.shape[1]).astype(BF16), values)
         return l, o.reshape(8, 16, 128)
+
+    def attend(blocks):
+        scored = [scores_of(keys, count) for keys, _, count in blocks]
+        m_old = m_acc[...]
+        m = m_old
+        for s in scored:
+            m = jnp.maximum(m, jnp.max(s, axis=2, keepdims=True))
+        alpha = jnp.exp(m_old - m)
+        l_sum = l_acc[...] * alpha
+        o_sum = o_acc[...] * alpha
+        for s, (_, values, count) in zip(scored, blocks):
+            l, o = weigh(s, count, m, values)
+            l_sum += l
+            o_sum += o
+        m_acc[...] = m
+        l_acc[...] = l_sum
+        o_acc[...] = o_sum
+
+    def attend_new(lo, hi):
+        attend(
+            [(kv[0, i, lo:hi, :], kv[1, i, lo:hi, :], counts[i, :, lo:hi]) for i in range(n_dp)]
+        )
 
     for g in range(8):
         qs[g * 16 : (g + 1) * 16, :] = queries[:, g * 128 : (g + 1) * 128]
@@ -291,37 +352,40 @@
         cols = pl.ds(pl.multiple_of(b * BLOCK, BLOCK), BLOCK)
         lane = lax.broadcasted_iota(jnp.int32, (16, BLOCK), 1)
         count = count_of((lane + b * BLOCK) // PAGE)
-        s = scores_of(cache[cols, :128], count)
-        m_old = m_acc[...]
-        m = jnp.maximum(m_old, jnp.max(s, axis=2, keepdims=True))
-        l, o = weigh(s, count, m, cache[cols, 128:])
-        alpha = jnp.exp(m_old - m)
-        m_acc[...] = m
-        l_acc[...] = l_acc[...] * alpha + l
-        o_acc[...] = o_acc[...] * alpha + o
+        attend([(cache[cols, :128], cache[cols, 128:], count)])
+
+    swap_shrink(1 - kind).wait_recv()
+    shp[my_y] = pair[0] + pair[1]
+    for y in range(1, n_y):
+        for other in (0, 1):
+            to_shrink(y, other).start()
 
     for d in range(1, n_dp):
         from_slots(d).wait_recv()
     new_pages = tok // PAGE // 2
+    owner_page = lax.broadcasted_iota(jnp.int32, (tok, 128), 0) // PAGE
+    spread_pages = jnp.where(
+        owner_page == lax.broadcasted_iota(jnp.int32, owner_page.shape, 1), 1.0, 0.0
+    )
 
     @pl.loop(0, n_dp)
     def _(i):
-        dest = slots_all[i, 0:1, :]
+        dest = exact_nt(slots_all[i].astype(F32), spread_pages).astype(jnp.int32)[0:1, :]
         mine = dest // new_pages == dp * 2 + kind
         page_ids = jnp.where(mine, dest % new_pages + pool, -1)
         counts[i] = count_of(page_ids)
 
-    for d in range(1, n_tp):
-        from_shrink(d).wait_recv()
+    for y in range(1, n_y):
+        for other in (0, 1):
+            from_shrink(y, other).wait_recv()
     total = shp[0]
-    for t in range(1, n_tp):
+    for t in range(1, n_y):
         total = total + shp[t]
     shrink[...] = total.astype(BF16).astype(F32)
     for load in loads[2:]:
         load.wait()
 
-    @pl.loop(0, n_chunk)
-    def _(k):
+    def near_part(k):
         cols = rows(k)
         from_sibling(k).wait_recv()
         low = jnp.broadcast_to(shrink[:, cols][None], (tenants, 16, CHUNK))
@@ -333,15 +397,9 @@
         for src in (me, sib):
             acc_kv += dot(xg[src, cols, :], wkv[src])
             acc_q[...] += dot(xg[src, cols, :], wq[src])
-        for y in range(1, n_y):
-            from_far(k, y).wait_recv()
-            pass_on(k, y).start()
-
-        @pl.when(k + 2 < n_chunk)
-        def _():
-            for y in range(1, n_y):
-                to_far(k + 2, y).start()
-
+        return acc_kv
+
+    def far_keys(k, cols, acc_kv):
         for y in range(1, n_y):
             src = far_from(y)
             acc_kv += dot(xg[src, cols, :], wkv[src])
@@ -352,6 +410,9 @@
         kv[kind, dp, cols, :] = acc_kv.astype(BF16)
         for other, d in page_pairs():
             to_pages(k, other, d).start()
+
+    def far_queries(k):
+        cols = rows(k)
         for y in range(1, n_y):
             for base in (me, sib):
                 src = lax.rem(base + n_tp - 2 * y, n_tp)
@@ -359,40 +420,78 @@
         oq[cols, :] = acc_q[...].astype(BF16)
         pltpu.make_async_copy(oq.at[cols], out_q.at[cols], out_sem.at[k]).start()
 
-    @pl.loop(0, n_chunk)
+    def arrive(k):
+        for y in range(1, n_y):
+            from_far(k, y).wait_recv()
+            pass_on(k, y).start()
+
+    @pl.loop(0, last)
+    def _(k):
+        acc_kv = near_part(k)
+        arrive(k)
+
+        @pl.when(k + AHEAD < last)
+        def _():
+            for y in range(1, n_y):
+                to_far(k + AHEAD, y).start()
+
+        for u in range(AHEAD):
+
+            @pl.when(k == last - AHEAD + u)
+            def _():
+                for y in range(1, n_y):
+                    to_far(last + u, y).start()
+
+        far_keys(k, rows(k), acc_kv)
+        far_queries(k)
+
+    acc_last = near_part(last)
+
+    @pl.loop(0, last)
     def _(k):
         for other, d in page_pairs():
             from_pages(k, other, d).wait_recv()
 
-    parts = [scores_of(kv[0, i], counts[i]) for i in range(n_dp)]
-    m_old = m_acc[...]
-    m = m_old
-    for s in parts:
-        m = jnp.maximum(m, jnp.max(s, axis=2, keepdims=True))
-    alpha = jnp.exp(m_old - m)
-    l_sum = l_acc[...] * alpha
-    o_sum = o_acc[...] * alpha
-    for i, s in enumerate(parts):
-        l, o = weigh(s, counts[i], m, kv[1, i])
-        l_sum += l
-        o_sum += o
-    result = (o_sum / l_sum).astype(BF16)
+    attend_new(0, last * CHUNK)
+    for u in range(n_sub):
+        arrive(last + u)
+        if u + AHEAD < n_sub:
+            for y in range(1, n_y):
+                to_far(last + u + AHEAD, y).start()
+        far_keys(last + u, unit_rows(last + u), acc_last[u * SUB : (u + 1) * SUB])
+    far_queries(last)
+    for u in range(n_sub):
+        for other, d in page_pairs():
+            from_pages(last + u, other, d).wait_recv()
+    attend_new(last * CHUNK, tok)
+    result = (o_acc[...] / l_acc[...]).astype(BF16)
     for g in range(8):
         out_a[:, g * 128 : (g + 1) * 128] = result[g]
 
     for d in range(1, n_dp):
         to_slots(d).wait_send()
-    for d in range(1, n_tp):
-        to_shrink(d).wait_send()
-
-    @pl.loop(0, n_chunk)
-    def _(k):
-        to_sibling(k).wait_send()
+    swap_shrink(kind).wait_send()
+    for y in range(1, n_y):
+        for other in (0, 1):
+            to_shrink(y, other).wait_send()
+
+    def finish(k):
         for y in range(1, n_y):
             to_far(k, y).wait_send()
             pass_on(k, y).wait_send()
         for other, d in page_pairs():
             to_pages(k, other, d).wait_send()
+
+    @pl.loop(0, last)
+    def _(k):
+        finish(k)
+
+    for u in range(n_sub):
+        finish(last + u)
+
+    @pl.loop(0, n_chunk)
+    def _(k):
+        to_sibling(k).wait_send()
         pltpu.make_async_copy(oq.at[rows(k)], out_q.at[rows(k)], out_sem.at[k]).wait()
 
 
@@ -421,19 +520,18 @@
     half = queries.shape[2]
     n_chunk = tok // CHUNK
     down = adapter_down_weight.transpose(1, 2, 0).reshape(ranks, feat)
-    slots = jnp.broadcast_to(jnp.repeat(page_destination_slot, PAGE)[None, :], (8, tok))
-    meta = jnp.concatenate([request_page_table, context_length[:, None]], axis=1)
     hbm = pl.BlockSpec(memory_space=pl.ANY)
     vmem = pl.BlockSpec(memory_space=pltpu.VMEM)
     dma = pltpu.SemaphoreType.DMA
     n_far = n_tp // 2 - 1
+    n_unit = n_chunk - 1 + CHUNK // SUB
     out_a, out_q = pl.pallas_call(
         functools.partial(kernel, n_tp, n_dp, pool),
         out_shape=(
             jax.ShapeDtypeStruct((half, queries.shape[3]), BF16),
             jax.ShapeDtypeStruct((tok, qcols), BF16),
         ),
-        in_specs=[hbm] * 6 + [vmem] * 3 + [hbm, vmem],
+        in_specs=[hbm] * 6 + [vmem] * 4 + [hbm, vmem],
         out_specs=(vmem, hbm),
         scratch_shapes=[
             pltpu.VMEM((n_tp, tok, feat), BF16),
@@ -445,9 +543,11 @@
             pltpu.VMEM((pool * PAGE, 2 * head), BF16),
             pltpu.VMEM((tok, qcols), BF16),
             pltpu.VMEM((2, n_dp, tok, head), BF16),
-            pltpu.VMEM((n_tp, rank, tok), F32),
+            pltpu.VMEM((2, rank, tok), F32),
+            pltpu.VMEM((n_tp // 2, rank, tok), F32),
             pltpu.VMEM((rank, tok), F32),
-            pltpu.VMEM((n_dp, 8, tok), jnp.int32),
+            pltpu.VMEM((n_dp, 8, 128), jnp.int32),
+            pltpu.VMEM((8, 128), jnp.int32),
             pltpu.VMEM((n_dp, half, tok), F32),
             pltpu.VMEM((8 * half, head), BF16),
             pltpu.VMEM((8, half, head), F32),
@@ -458,16 +558,18 @@
             dma,
             dma((n_chunk,)),
             dma((n_chunk,)),
-            dma((n_chunk, n_far)),
-            dma((n_chunk, n_far)),
-            dma((n_chunk, n_far)),
-            dma((n_chunk, n_far)),
-            dma((n_tp - 1,)),
-            dma((n_tp - 1,)),
+            dma((n_unit, n_far)),
+            dma((n_unit, n_far)),
+            dma((n_unit, n_far)),
+            dma((n_unit, n_far)),
+            dma,
+            dma,
+            dma((2 * n_far,)),
+            dma((2 * n_far,)),
             dma((n_dp - 1,)),
             dma((n_dp - 1,)),
-            dma((n_chunk, 2 * n_dp)),
-            dma((n_chunk, 2 * n_dp)),
+            dma((n_unit, 2 * n_dp)),
+            dma((n_unit, 2 * n_dp)),
             dma((n_chunk,)),
         ],
         compiler_params=pltpu.CompilerParams(
@@ -482,8 +584,9 @@
         query_up_weight.reshape(ranks, qcols),
         adapter_up_weight.reshape(ranks, head),
         tenant[None, :],
-        slots,
-        meta,
+        page_destination_slot[None, :],
+        request_page_table.T,
+        context_length[None, :],
         key_value_cache.reshape(pool * PAGE, 2 * head),
         queries.reshape(half, -1),
     )

time: 125 us -> 121 us (0.968)
  local copies, waits for them, and re-layouts: 7.39 us -> 4.45 us
    broadcast_in_dim x4 -> x0, local copies, waits for them, and re-layouts: 2.17 us -> none  [the longest x1 0.74 us: per_device(): context_length[:, None]]
    pallas_call x1, Pallas kernels: 116 us -> 115 us  [per_device(): pl.pallas_call(functools.partial(kernel, n_tp, n_dp, pool), out_shape=(ja...]
    unnamed x3 -> x2, local copies, waits for them, and re-layouts: 5.23 us -> 4.45 us
where the time goes in v2:
time: 121 us; the launch traced here: 120 us
  Pallas kernels  115 us (95%)
  local copies, waits for them, and re-layouts  4.45 us (4%)
    pallas_call x1, Pallas kernels, per_device(): pl.pallas_call(functools.partial(kernel, n_tp, n_dp, pool), out_shape=(ja...  115 us
    unnamed x2, local copies, waits for them, and re-layouts  4.45 us

profile of v2, /device:TPU:1, one launch (start us, length us, event | category | flops | bytes accessed | tf_op | source)
XLA Modules:
  0.0 120.1 jit_solution(5393525189014217708)
XLA Ops:
  0.6 115.0 %serve_layer.1 = (bf16[16,1024]{1,0:T(8,128)(2,1)}, bf16[1024,1024]{1,0:T(8,128)(2,1)}) custom-call(bf16[1024,2048]{1,0:T(8,128)(2,1)} %x_hbm.1, bf16[4,2048,1024]{2,1,0:T(8,128)(2,1)} %bitcast.14, bf16[4,2048,128]{2,1,0:T(8,128)(2,1)} %bitcast.16, bf16[1024,2048]{1,0:T(8,128)(2,1)} %bitcast.15, bf16[1024,1024]{1,0:T(8,128)(2,1)} %bitcast.17, ...), custom_call_target="tpu_custom_call" | custom-call | tf_op jit(solution)/shard_map/serve_layer/pallas_call | solution.py:528
  115.6 1.4 %copy.16 = bf16[1,1,16,1024]{3,2,1,0:T(8,128)(2,1)} copy(bf16[1,1,16,1024]{3,2,1,0:T(8,128)(2,1)} %bitcast.21) | data formatting | bytes 65536
  117.0 3.1 %copy.17 = bf16[1024,1024]{1,0:T(8,128)(2,1)} copy(bf16[1024,1024]{1,0:T(8,128)(2,1)} %get-tuple-element.9) | data formatting | bytes 4194304

commit v3 on v2

--- a/solution.py
+++ b/solution.py
@@ -10,8 +10,8 @@
 
 PAGE = 16
 CHUNK = 128
-SUB = 32
-AHEAD = 3
+SUB = 64
+AHEAD = 4
 BLOCK = 1024
 NEG = -1e30
 F32 = jnp.float32
@@ -435,7 +435,7 @@
             for y in range(1, n_y):
                 to_far(k + AHEAD, y).start()
 
-        for u in range(AHEAD):
+        for u in range(min(AHEAD, n_sub)):
 
             @pl.when(k == last - AHEAD + u)
             def _():

time: 121 us -> 119 us (0.983)
  Pallas kernels: 115 us -> 113 us
    pallas_call x1, Pallas kernels: 115 us -> 113 us  [per_device(): pl.pallas_call(functools.partial(kernel, n_tp, n_dp, pool), out_shape=(ja...]
where the time goes in v3:
time: 119 us
  Pallas kernels  113 us (95%)
  local copies, waits for them, and re-layouts  4.45 us (4%)
    pallas_call x1, Pallas kernels, per_device(): pl.pallas_call(functools.partial(kernel, n_tp, n_dp, pool), out_shape=(ja...  113 us
    unnamed x2, local copies, waits for them, and re-layouts  4.45 us

profile of v3, /device:TPU:1, one launch (start us, length us, event | category | flops | bytes accessed | tf_op | source)
XLA Modules:
  0.0 118.6 jit_solution(9771512503972804422)
XLA Ops:
  0.6 113.5 %serve_layer.1 = (bf16[16,1024]{1,0:T(8,128)(2,1)}, bf16[1024,1024]{1,0:T(8,128)(2,1)}) custom-call(bf16[1024,2048]{1,0:T(8,128)(2,1)} %x_hbm.1, bf16[4,2048,1024]{2,1,0:T(8,128)(2,1)} %bitcast.14, bf16[4,2048,128]{2,1,0:T(8,128)(2,1)} %bitcast.16, bf16[1024,2048]{1,0:T(8,128)(2,1)} %bitcast.15, bf16[1024,1024]{1,0:T(8,128)(2,1)} %bitcast.17, ...), custom_call_target="tpu_custom_call" | custom-call | tf_op jit(solution)/shard_map/serve_layer/pallas_call | solution.py:528
  114.1 1.4 %copy.16 = bf16[1,1,16,1024]{3,2,1,0:T(8,128)(2,1)} copy(bf16[1,1,16,1024]{3,2,1,0:T(8,128)(2,1)} %bitcast.21) | data formatting | bytes 65536
  115.5 3.1 %copy.17 = bf16[1024,1024]{1,0:T(8,128)(2,1)} copy(bf16[1024,1024]{1,0:T(8,128)(2,1)} %get-tuple-element.9) | data formatting | bytes 4194304
